TPU v7x, 32 devices: a whole 2x2x4 slice. The times are simulated.
32 devices in a mesh: dp: 4 (over x, core), ctx: 8 (over z, y).
Axes of the slice: x: 2, y: 2, z: 4, core: 2. Of those that a mesh axis runs over, the one named last changes fastest.
Arguments:
- tokens: bfloat16 [4, 2, 8, 64, 2048], P('dp', None, 'ctx'), may hold values from -6 to 6
- norm_gain: bfloat16 [2048], P(('dp', 'ctx')), may hold values from 0.5 to 1.5
- norm_shift: bfloat16 [2048], P(('dp', 'ctx')), may hold values from -0.5 to 0.5
- input_weight: bfloat16 [2048, 14336], P(('dp', 'ctx')), may hold values from -0.1875 to 0.1875
- input_bias: bfloat16 [14336], P(('dp', 'ctx')), may hold values from -0.5 to 0.5
- output_weight: bfloat16 [10240, 2048], P(('dp', 'ctx')), may hold values from -0.0625 to 0.0625
- output_bias: bfloat16 [2048], P(('dp', 'ctx')), may hold values from -0.5 to 0.5
- cotangent: bfloat16 [4, 2, 8, 64, 2048], P('dp', None, 'ctx'), may hold values from -6 to 6
Outputs:
- block_out: bfloat16 [4, 2, 8, 64, 2048], P('dp', None, 'ctx')
- tokens_grad: float32 [4, 2, 8, 64, 2048], P('dp', None, 'ctx')
- gain_grad: float32 [2048], P(('dp', 'ctx'))
- shift_grad: float32 [2048], P(('dp', 'ctx'))
- weightin_grad: float32 [2048, 14336], P(('dp', 'ctx'))
- biasin_grad: float32 [14336], P(('dp', 'ctx'))
- weightout_grad: float32 [10240, 2048], P(('dp', 'ctx'))
- biasout_grad: float32 [2048], P(('dp', 'ctx'))
All inputs are finite; a program needn't handle non-finite values.
Results may differ from a plain program's by a relative error of at most 0.0081.
Values may be sent and summed in bfloat16 or wider, within the bound.
No kernel may reach another device: no remote copies, remote signals or barrier semaphores. Data moves between devices by JAX's collectives and lax.ppermute only.
A program may use at most 512 MiB of HBM per device.

v0:
```python
import math

import jax
import jax.numpy as jnp
from jax import lax
from jax.sharding import PartitionSpec as P

D = 2048
HEADS = 32
HEAD = 64
ROT = 32
BLK = 64


epsilon = 1e-05
theta_log = math.log(10000.0)
masked_fill = -1e30


def layer_norm(values, norm_gain, norm_shift):
    middle = jnp.mean(values, axis=-1, keepdims=True)
    centred = values - middle
    spread = jnp.mean(centred * centred, axis=-1, keepdims=True)
    return centred * lax.rsqrt(spread + epsilon) * norm_gain + norm_shift


def turn_heads(values, angles):
    half_rot = ROT // 2
    former = values[..., :half_rot]
    latter = values[..., half_rot:ROT]
    cosine = jnp.cos(angles)[:, None, :]
    sine_table = jnp.sin(angles)[:, None, :]
    return jnp.concatenate(
        [
            former * cosine - latter * sine_table,
            latter * cosine + former * sine_table,
            values[..., ROT:],
        ],
        axis=-1,
    )


def angle_table(positions):
    frequency = jnp.exp(-theta_log * 2.0 * jnp.arange(ROT // 2).astype(jnp.float32) / ROT)
    return positions.astype(jnp.float32)[:, None] * frequency[None, :]


def gelu_tanh(values):
    return jax.nn.gelu(values, approximate=True)


def head_scores(queries, key_part):
    raw = jnp.einsum("sqge,csbtge->sgqcbt", queries, key_part, preferred_element_type=jnp.float32)
    return raw.reshape(raw.shape[0], raw.shape[1], raw.shape[2], -1) * 0.125


def local(
    tokens, norm_gain, norm_shift, input_weight, input_bias, output_weight, output_bias, cotangent
):
    ctx_count = lax.axis_size("ctx")
    ctx_place = lax.axis_index("ctx")
    seq_local = tokens.shape[0]
    local_rows = 2 * BLK
    row_count = seq_local * local_rows
    group = math.gcd(HEADS, 8)
    group_count = HEADS // group
    flat_in = tokens.reshape(row_count, D).astype(jnp.float32)
    weight_entry, bias_entry, gain_full, shift_full = (
        lax.all_gather(input_weight, ("dp", "ctx"), axis=0, tiled=True),
        lax.all_gather(input_bias, ("dp", "ctx"), axis=0, tiled=True),
        lax.all_gather(norm_gain, ("dp", "ctx"), axis=0, tiled=True),
        lax.all_gather(norm_shift, ("dp", "ctx"), axis=0, tiled=True),
    )
    normed, norm_back = jax.vjp(
        layer_norm, flat_in, gain_full.astype(jnp.float32), shift_full.astype(jnp.float32)
    )
    normed_low = normed.astype(jnp.bfloat16)
    hidden = jnp.dot(
        normed_low, weight_entry, preferred_element_type=jnp.float32
    ) + bias_entry.astype(jnp.float32)
    halves = jnp.arange(2, dtype=jnp.int32)
    within = jnp.arange(BLK, dtype=jnp.int32)
    query_pos = (
        ((ctx_place + halves * (2 * ctx_count - 1 - 2 * ctx_place)) * BLK)[:, None]
        + within[None, :]
    ).reshape(local_rows)
    slots = jnp.arange(ctx_count, dtype=jnp.int32)
    key_start = (slots[:, None] + halves[None, :] * (2 * ctx_count - 1 - 2 * slots[:, None])) * BLK
    key_table = (key_start[:, :, None] + within[None, None, :]).reshape(ctx_count, local_rows)
    key_pos = key_table.reshape(ctx_count * local_rows)
    angles = angle_table(jnp.tile(query_pos, seq_local))

    def rotate_rows(flat_part):
        return turn_heads(flat_part.reshape(row_count, HEADS, HEAD), angles)

    query_turned, turn_back = jax.vjp(rotate_rows, hidden[:, :D])
    key_turned = rotate_rows(hidden[:, D : 2 * D])
    query_low = query_turned.astype(jnp.bfloat16).reshape(seq_local, local_rows, HEADS, HEAD)
    key_low = key_turned.astype(jnp.bfloat16).reshape(row_count, D)
    value_low = hidden[:, 2 * D : 3 * D].astype(jnp.bfloat16)
    pair_local = jnp.concatenate([key_low, value_low], axis=-1).reshape(1, seq_local, 2, BLK, 2 * D)
    pair_all = lax.all_gather(pair_local, "ctx", axis=0, tiled=True)
    pair_view = pair_all.reshape(ctx_count, seq_local, 2, BLK, 2, HEADS, HEAD)
    allowed = key_pos[None, :] <= query_pos[:, None]

    def head_slice(which, start):
        piece = lax.dynamic_slice(
            pair_view, (0, 0, 0, 0, which, start, 0), (ctx_count, seq_local, 2, BLK, 1, group, HEAD)
        )
        return piece.reshape(ctx_count, seq_local, 2, BLK, group, HEAD)

    def forward_group(index):
        start = index * group
        queries = lax.dynamic_slice_in_dim(query_low, start, group, 2)
        key_part = head_slice(0, start)
        value_part = head_slice(1, start)
        scores = jnp.where(allowed, head_scores(queries, key_part), masked_fill)
        row_top = jnp.max(scores, axis=-1, keepdims=True)
        weights = jnp.exp(scores - row_top)
        totals = jnp.sum(weights, axis=-1, keepdims=True)
        shares = (weights / totals).astype(jnp.bfloat16)
        shares = shares.reshape(seq_local, group, local_rows, ctx_count, 2, BLK)
        mixture = jnp.einsum(
            "sgqcbt,csbtge->sqge", shares, value_part, preferred_element_type=jnp.float32
        )
        return (mixture, row_top[..., 0] + jnp.log(totals[..., 0]))

    group_ids = jnp.arange(group_count, dtype=jnp.int32)
    mixtures, lse_groups = lax.map(forward_group, group_ids)
    attended_low = jnp.moveaxis(mixtures, 0, 2).reshape(row_count, D).astype(jnp.bfloat16)
    activated, gelu_back = jax.vjp(gelu_tanh, hidden[:, 3 * D :])
    branch_low = jnp.concatenate([attended_low, activated.astype(jnp.bfloat16)], axis=-1)
    weight_exit, bias_exit = (
        lax.all_gather(output_weight, ("dp", "ctx"), axis=0, tiled=True),
        lax.all_gather(output_bias, ("dp", "ctx"), axis=0, tiled=True),
    )
    block_out = (
        (
            flat_in
            + jnp.dot(branch_low, weight_exit, preferred_element_type=jnp.float32)
            + bias_exit.astype(jnp.float32)
        )
        .astype(jnp.bfloat16)
        .reshape(tokens.shape)
    )
    weight_entry, weight_exit = (
        lax.all_gather(input_weight, ("dp", "ctx"), axis=0, tiled=True),
        lax.all_gather(output_weight, ("dp", "ctx"), axis=0, tiled=True),
    )
    grad_out = cotangent.reshape(row_count, D)
    grad_branch = lax.dot_general(
        grad_out, weight_exit, (((1,), (1,)), ((), ())), preferred_element_type=jnp.float32
    )
    exit_weight_term = lax.dot_general(
        branch_low, grad_out, (((0,), (0,)), ((), ())), preferred_element_type=jnp.float32
    )
    exit_bias_term = jnp.sum(grad_out.astype(jnp.float32), axis=0)
    weightout_grad, biasout_grad = (
        lax.psum_scatter(exit_weight_term, ("dp", "ctx"), scatter_dimension=0, tiled=True),
        lax.psum_scatter(exit_bias_term, ("dp", "ctx"), scatter_dimension=0, tiled=True),
    )
    grad_mix = grad_branch[:, :D].astype(jnp.bfloat16).reshape(seq_local, local_rows, HEADS, HEAD)
    (grad_up,) = gelu_back(grad_branch[:, D:])

    def query_group(index):
        start = index * group
        queries = lax.dynamic_slice_in_dim(query_low, start, group, 2)
        grad_part = lax.dynamic_slice_in_dim(grad_mix, start, group, 2)
        key_part = head_slice(0, start)
        value_part = head_slice(1, start)
        scores = jnp.where(allowed, head_scores(queries, key_part), masked_fill)
        shares = jnp.exp(scores - lse_groups[index][..., None])
        grad_shares = head_scores(grad_part, value_part) * 8.0
        inner = jnp.sum(shares * grad_shares, axis=-1)
        grad_scores = (shares * (grad_shares - inner[..., None])).astype(jnp.bfloat16)
        grad_scores = grad_scores.reshape(seq_local, group, local_rows, ctx_count, 2, BLK)
        grad_query = (
            jnp.einsum(
                "sgqcbt,csbtge->sqge", grad_scores, key_part, preferred_element_type=jnp.float32
            )
            * 0.125
        )
        return (grad_query, inner)

    grad_queries, inner_groups = lax.map(query_group, group_ids)
    grad_query_rows = jnp.moveaxis(grad_queries, 0, 2).reshape(row_count, HEADS, HEAD)
    lse_heads = jnp.moveaxis(lse_groups, 0, 1).reshape(seq_local, HEADS, local_rows)
    inner_heads = jnp.moveaxis(inner_groups, 0, 1).reshape(seq_local, HEADS, local_rows)
    stride = math.gcd(1 * lax.axis_size("ctx"), 4)

    def slot_group(index):
        piece = lax.dynamic_slice_in_dim(pair_view, index * stride, stride, 0)
        piece_pos = lax.dynamic_slice_in_dim(key_table, index * stride, stride, 0).reshape(
            stride * local_rows
        )
        key_part = piece[:, :, :, :, 0]
        value_part = piece[:, :, :, :, 1]
        fits = piece_pos[None, :] <= query_pos[:, None]
        scores = jnp.where(fits, head_scores(query_low, key_part), masked_fill)
        shares = jnp.exp(scores - lse_heads[..., None])
        grad_shares = head_scores(grad_mix, value_part) * 8.0
        grad_scores = (shares * (grad_shares - inner_heads[..., None])).astype(jnp.bfloat16)
        grad_scores = grad_scores.reshape(seq_local, HEADS, local_rows, stride, 2, BLK)
        shares_low = shares.astype(jnp.bfloat16).reshape(
            seq_local, HEADS, local_rows, stride, 2, BLK
        )
        grad_values = jnp.einsum(
            "sgqcbt,sqge->csbtge", shares_low, grad_mix, preferred_element_type=jnp.float32
        )
        grad_keys = (
            jnp.einsum(
                "sgqcbt,sqge->csbtge", grad_scores, query_low, preferred_element_type=jnp.float32
            )
            * 0.125
        )
        return jnp.stack([grad_keys, grad_values], axis=4).reshape(stride, seq_local, 2, BLK, 2 * D)

    terms = lax.map(slot_group, jnp.arange(1 * lax.axis_size("ctx") // stride, dtype=jnp.int32))
    pair_grad = lax.psum_scatter(
        terms.reshape(1 * lax.axis_size("ctx"), seq_local, 2, BLK, 2 * D),
        "ctx",
        scatter_dimension=0,
        tiled=True,
    )
    pair_rows = pair_grad.reshape(row_count, 2 * D)
    (grad_query_in,) = turn_back(grad_query_rows)
    (grad_key_in,) = turn_back(pair_rows[:, :D].reshape(row_count, HEADS, HEAD))
    grad_hidden = jnp.concatenate(
        [grad_query_in, grad_key_in, pair_rows[:, D:], grad_up], axis=-1
    ).astype(jnp.bfloat16)
    entry_weight_term = lax.dot_general(
        normed_low, grad_hidden, (((0,), (0,)), ((), ())), preferred_element_type=jnp.float32
    )
    entry_bias_term = jnp.sum(grad_hidden.astype(jnp.float32), axis=0)
    grad_normed = lax.dot_general(
        grad_hidden, weight_entry, (((1,), (1,)), ((), ())), preferred_element_type=jnp.float32
    )
    grad_flat, gain_term, shift_term = norm_back(grad_normed)
    tokens_grad = (grad_out.astype(jnp.float32) + grad_flat).reshape(tokens.shape)
    weightin_grad, biasin_grad, gain_grad, shift_grad = (
        lax.psum_scatter(entry_weight_term, ("dp", "ctx"), scatter_dimension=0, tiled=True),
        lax.psum_scatter(entry_bias_term, ("dp", "ctx"), scatter_dimension=0, tiled=True),
        lax.psum_scatter(gain_term, ("dp", "ctx"), scatter_dimension=0, tiled=True),
        lax.psum_scatter(shift_term, ("dp", "ctx"), scatter_dimension=0, tiled=True),
    )
    return (
        block_out,
        tokens_grad,
        gain_grad,
        shift_grad,
        weightin_grad,
        biasin_grad,
        weightout_grad,
        biasout_grad,
    )


def solution(mesh):
    placed = (
        P("dp", None, "ctx", None, None),
        P(("dp", "ctx")),
        P(("dp", "ctx")),
        P(("dp", "ctx"), None),
        P(("dp", "ctx")),
        P(("dp", "ctx"), None),
        P(("dp", "ctx")),
        P("dp", None, "ctx", None, None),
    )
    return jax.shard_map(
        local,
        mesh=mesh,
        in_specs=placed,
        out_specs=(
            P("dp", None, "ctx", None, None),
            P("dp", None, "ctx", None, None),
            P(("dp", "ctx")),
            P(("dp", "ctx")),
            P(("dp", "ctx"), None),
            P(("dp", "ctx")),
            P(("dp", "ctx"), None),
            P(("dp", "ctx")),
        ),
        check_vma=False,
    )
```

profile of v0, /device:TPU:0, one launch (start us, length us, event | category | flops | bytes accessed | tf_op | source)
XLA Modules:
  0.0 5614.2 jit_solution(13448713797977692632)
XLA Ops:
  13.2 46.0 all-reduce.16
  60.3 270.3 %all-gather.4.cloned.1.call-done = bf16[2048,14336]{1,0:T(8,128)(2,1)} async-done(((bf16[64,14336]{1,0:T(8,128)(2,1)}), bf16[2048,14336]{1,0:T(8,128)(2,1)}) %all-gather.4.cloned.1.call-update) | async-done | bytes 58720272 | tf_op jit(solution)/shard_map/all_gather | solution.py:69
  330.6 24.9 convolution_add_fusion
  365.5 201.5 %all-gather.8.cloned.1.call-done = bf16[10240,2048]{1,0:T(8,128)(2,1)} async-done(((bf16[320,2048]{1,0:T(8,128)(2,1)}), bf16[10240,2048]{1,0:T(8,128)(2,1)}) %all-gather.8.cloned.1.call-update) | async-done | bytes 41943056 | tf_op jit(solution)/shard_map/all_gather | solution.py:134
  567.0 21.7 fusion.118
  591.4 101.4 %all-gather.6.cloned.1.call-done = bf16[8,1,2,64,4096]{4,3,2,1,0:T(8,128)(2,1)} async-done(((bf16[1,1,2,64,4096]{4,3,2,1,0:T(8,128)(2,1)}), bf16[8,1,2,64,4096]{4,3,2,1,0:T(8,128)(2,1)}) %all-gather.6.cloned.1.call-update) | async-done | bytes 8388624 | tf_op jit(solution)/shard_map/all_gather | solution.py:102
  692.7 23.6 reshape.568
  716.3 15.2 copy.70
  731.5 47.3 while.44
  778.9 51.0 while.45
  829.8 120.5 %while.46 = (s32[]{:T(128)}, f32[2,4,1,2,64,4096]{5,4,3,1,2,0:T(8,128)}, s32[2]{0:T(128)S(1)}, s32[8,128]{1,0:T(8,128)S(1)}, bf16[8,1,2,64,2,32,64]{6,3,2,0,5,4,...) while((s32[]{:T(128)}, ...), condition=%wide.region_10.11_spmd.clone.clone, body=%wide.region_9.10_spmd.clone.sunk.clone | while | flops 1097924736 | bytes 128184560 | solution.py:218
  838.4 8.4 multiply_bitcast_fusion.3
  855.9 11.9 copy.134
  867.8 14.7 broadcast_in_dim.189
  916.1 11.9 copy.134
  927.9 14.7 broadcast_in_dim.189
  961.3 270.0 %reduce-scatter.7.cloned.1.call-done = f32[1,1,2,64,4096]{4,3,2,1,0:T(8,128)} async-done(((f32[8,1,2,64,4096]{4,3,2,1,0:T(8,128)}), f32[1,1,2,64,4096]{4,3,2,1,0:T(8,128)}) %reduce-scatter.7.cloned.1.call-update) | async-done | bytes 2097168 | tf_op jit(solution)/shard_map/reduce_scatter | solution.py:219
  1250.0 27.8 fusion.115
  1280.2 30.1 fusion.106
  1310.4 42.1 fusion.113
  1353.2 16.8 fusion.105
  1372.7 28.0 all-reduce.19.cloned.1.call-done
  1405.8 1750.4 %reduce-scatter.9.cloned.1.call-done = f32[320,2048]{1,0:T(8,128)} async-done(((f32[10240,2048]{1,0:T(8,128)}), f32[320,2048]{1,0:T(8,128)}) %reduce-scatter.9.cloned.1.call-update) | async-done | bytes 2621456 | tf_op jit(solution)/shard_map/reduce_scatter | solution.py:159
  3156.2 2450.9 %reduce-scatter.11.cloned.1.call-done = f32[64,14336]{1,0:T(8,128)} async-done(((f32[2048,14336]{1,0:T(8,128)}), f32[64,14336]{1,0:T(8,128)}) %reduce-scatter.11.cloned.1.call-update) | async-done | bytes 3670032
  (259 shorter events, 202.2 us)
Async XLA Ops:
  7.2 52.7 copy-start.2
  7.2 323.4 %all-gather.4.cloned.1.call-start = ((), (), s32[]{:S(2)}) async-start(), calls=%async_computation.3 | async-start | bytes 60555264 | tf_op jit(solution)/shard_map/all_gather | solution.py:69
  8.0 559.0 %all-gather.8.cloned.1.call-start = ((), (), s32[]{:S(2)}) async-start(), calls=%async_computation.5 | async-start | bytes 43253760 | tf_op jit(solution)/shard_map/all_gather | solution.py:134
  8.7 684.0 %all-gather.6.cloned.1.call-start = ((), (), s32[]{:S(2)}) async-start(), calls=%async_computation.4 | async-start | bytes 9437184 | tf_op jit(solution)/shard_map/all_gather | solution.py:102
  10.0 345.5 %copy-start.18 = (f32[128]{0:T(128)}, f32[128]{0:T(128)S(1)}, u32[]{:S(2)}) copy-start(f32[128]{0:T(128)S(1)} %div.38) | copy-start | bytes 1540
  11.5 344.1 %copy-start.20 = (f32[128]{0:T(128)}, f32[128]{0:T(128)S(1)}, u32[]{:S(2)}) copy-start(f32[128]{0:T(128)S(1)} %rsqrt.10) | copy-start | bytes 1540
  12.2 47.6 copy-start.23
  59.9 300.2 %copy-start.13 = (f32[128,16]{0,1:T(8,128)}, f32[128,16]{0,1:T(8,128)S(1)}, u32[]{:S(2)}) copy-start(f32[128,16]{0,1:T(8,128)S(1)} %get-tuple-element.547) | copy-start | bytes 24580
  59.9 300.2 %copy-start.15 = (f32[128,16]{0,1:T(8,128)}, f32[128,16]{0,1:T(8,128)S(1)}, u32[]{:S(2)}) copy-start(f32[128,16]{0,1:T(8,128)S(1)} %get-tuple-element.548) | copy-start | bytes 24580
  60.3 295.2 %copy-start.6 = (bf16[128,2048]{1,0:T(8,128)(2,1)}, bf16[128,2048]{1,0:T(8,128)(2,1)S(1)}, u32[]{:S(2)}) copy-start(bf16[128,2048]{1,0:T(8,128)(2,1)S(1)} %add_convert_fusion.2) | copy-start | bytes 1572868
  360.3 206.7 %copy-start.4 = (bf16[1,2,1,64,2048]{4,3,2,1,0:T(8,128)(2,1)S(1)}, bf16[1,2,1,64,2048]{4,3,2,1,0:T(8,128)(2,1)}, u32[]{:S(2)}) copy-start(bf16[1,2,1,64,2048]{4,3,2,1,0:T(8,128)(2,1)} %param.21) | copy-start | bytes 1572868
  363.6 867.7 %reduce-scatter.7.cloned.1.call-start = ((), (), s32[]{:S(2)}) async-start(), calls=%async_computation.6 | async-start | bytes 18874368 | tf_op jit(solution)/shard_map/reduce_scatter | solution.py:219
  716.3 15.2 copy-start.17
  778.9 51.0 copy-start.32
  950.3 450.4 %all-reduce.19.cloned.1.call-start = ((), (), s32[]{:S(2)}) async-start(), calls=%async_computation.9 | async-start | bytes 163840
  958.4 279.8 %copy-start.14 = (f32[128,16]{0,1:T(8,128)S(1)}, f32[128,16]{0,1:T(8,128)}, u32[]{:S(2)}) copy-start(f32[128,16]{0,1:T(8,128)} %copy-done.13) | copy-start | bytes 24580
  958.4 279.8 %copy-start.16 = (f32[128,16]{0,1:T(8,128)S(1)}, f32[128,16]{0,1:T(8,128)}, u32[]{:S(2)}) copy-start(f32[128,16]{0,1:T(8,128)} %copy-done.15) | copy-start | bytes 24580
  1240.6 9.4 copy-start.3
  1240.6 9.4 copy-start.12
  1240.6 9.4 copy-start.19
  1250.0 27.8 copy-start.30
  1250.0 27.8 copy-start.21
  1280.2 1876.0 %reduce-scatter.9.cloned.1.call-start = ((), (), s32[]{:S(2)}) async-start(), calls=%async_computation.7 | async-start | bytes 86507520 | tf_op jit(solution)/shard_map/reduce_scatter | solution.py:159
  1310.4 4296.7 %reduce-scatter.11.cloned.1.call-start = ((), (), s32[]{:S(2)}) async-start(), calls=%async_computation.8 | async-start | bytes 121110528
  (26 other events, 81.1 us)
Sparse Core Ops, SparseCore 0:
  10.9 319.6 all-gather.3
  333.5 233.3 all-gather.7
  569.7 123.0 all-gather.5
  950.4 280.7 reduce-scatter.6
  1280.3 120.3 all-reduce.18
  1403.6 1752.5 reduce-scatter.8
  3159.2 2447.7 reduce-scatter.10
where the time goes:
time: 5620 us; the launch traced here: 5610 us
  waiting for transfers between devices  5070 us (90%)
  matrix products  259 us (5%)
  local copies, waits for them, and re-layouts  167 us (3%)
    unnamed x9, waiting for transfers between devices  2480 us
    reduce_scatter x1, waiting for transfers between devices, local(): lax.psum_scatter(exit_weight_term, ('dp', 'ctx'), scatter_dimension=0, ti...  1750 us
    all_gather x1, waiting for transfers between devices, local(): lax.all_gather(input_weight, ('dp', 'ctx'), axis=0, tiled=True)  270 us
    reduce_scatter x1, waiting for transfers between devices, local(): lax.psum_scatter(terms.reshape(1 * lax.axis_size('ctx'), seq_local, 2, BL...  270 us
    all_gather x1, waiting for transfers between devices, local(): lax.all_gather(output_weight, ('dp', 'ctx'), axis=0, tiled=True)  201 us
  transfers between devices with their start and end apart: 7, of which 7 were waited for; matrix products, arithmetic and copies ran while one was open for 3% of the time, Pallas kernels for 0%

commit v1 on v0

v1 whole, which is shorter than its diff:
```python
import functools
import math

import jax
import jax.numpy as jnp
from jax import lax
from jax.experimental import pallas as pl
from jax.experimental.pallas import tpu as pltpu
from jax.sharding import PartitionSpec as P

D = 2048
HEADS = 32
HEAD = 64
ROT = 32
BLK = 64
FF = 8192
TILE = 256

epsilon = 1e-05
theta_log = math.log(10000.0)
masked_fill = -1e30
bf16 = jnp.bfloat16
f32 = jnp.float32


def dot(a, b, dims):
    return lax.dot_general(a, b, (dims, ((), ())), preferred_element_type=f32)


def turn_lanes(values, cos, sin, lanes, sign):
    half = ROT // 2
    width = values.shape[-1]
    place = lanes % HEAD
    ahead = pltpu.roll(values, width - half, 1)
    behind = pltpu.roll(values, half, 1)
    turned = values * cos + sign * sin * jnp.where(place < half, -ahead, behind)
    return jnp.where(place < ROT, turned, values)


def attention_kernel(length, width, hq, hk, hv, gm, cos, sin, att, gq, gk, gv, qs, ks, vs, kt, vt, dk, dv):
    lanes = lax.broadcasted_iota(jnp.int32, (1, width), 1)
    tile = min(TILE, length)
    cos_all, sin_all = cos[...], sin[...]
    turn = functools.partial(turn_lanes, cos=cos_all, sin=sin_all, lanes=lanes)
    qs[...] = turn(hq[...], sign=1.0).astype(bf16)
    turned_keys = turn(hk[...], sign=1.0)
    ks[...] = turned_keys.astype(bf16)
    kt[...] = turned_keys.T.astype(bf16)
    values = hv[...]
    vs[...] = values.astype(bf16)
    vt[...] = values.T.astype(bf16)
    dk[...] = jnp.zeros_like(dk)
    dv[...] = jnp.zeros_like(dv)
    causal = lax.broadcasted_iota(jnp.int32, (tile, tile), 0) <= lax.broadcasted_iota(
        jnp.int32, (tile, tile), 1
    )

    def rows_step(start, reach):
        rows = pl.ds(start, tile)
        q_rows = qs[rows, :]
        g_rows = gm[rows, :]
        keys = ks[0:reach, :]
        vals = vs[0:reach, :]
        mixes, gqs = [], []
        if reach == tile:
            allowed = causal
        else:
            allowed = lax.broadcasted_iota(jnp.int32, (reach, tile), 0) <= start + (
                lax.broadcasted_iota(jnp.int32, (reach, tile), 1)
            )
        for head in range(width // HEAD):
            mine = (lanes // HEAD) == head
            q_head = jnp.where(mine, q_rows, jnp.zeros_like(q_rows))
            g_head = jnp.where(mine, g_rows, jnp.zeros_like(g_rows))
            span = slice(head * HEAD, (head + 1) * HEAD)
            scores = dot(keys, q_head, ((1,), (1,))) * 0.125
            scores = jnp.where(allowed, scores, masked_fill)
            top = jnp.max(scores, axis=0, keepdims=True)
            weights = jnp.exp(scores - top)
            total = jnp.sum(weights, axis=0, keepdims=True)
            shares = weights * (1.0 / total)
            low = shares.astype(bf16)
            grad_shares = dot(vals, g_head, ((1,), (1,)))
            moved = shares * grad_shares
            inner = jnp.sum(moved, axis=0, keepdims=True)
            grad_scores = (moved - shares * inner).astype(bf16)
            mixes.append(dot(vt[span, 0:reach], low, ((1,), (0,))))
            gqs.append(dot(kt[span, 0:reach], grad_scores, ((1,), (0,))))
            dv[0:reach, :] += dot(low, g_head, ((1,), (0,)))
            dk[0:reach, :] += dot(grad_scores, q_head, ((1,), (0,)))
        att[rows, :] = jnp.concatenate(mixes, axis=0).T.astype(bf16)
        grad_q = jnp.concatenate(gqs, axis=0).T * 0.125
        gq[rows, :] = turn_lanes(grad_q, cos[rows, :], sin[rows, :], lanes, -1.0).astype(bf16)

    count = length // tile
    if count <= 4:
        for step in range(count):
            rows_step(step * tile, (step + 1) * tile)
    else:
        per = count // 4
        for part in range(4):

            @pl.loop(part * per, (part + 1) * per)
            def _(step, part=part):
                rows_step(pl.multiple_of(step * tile, tile), (part + 1) * per * tile)

    gk[...] = turn(dk[...] * 0.125, sign=-1.0).astype(bf16)
    gv[...] = dv[...].astype(bf16)


def attention(hidden, grad_mix):
    length, columns = grad_mix.shape
    width = min(128, columns)
    groups = columns // width
    frequency = jnp.exp(-theta_log * 2.0 * jnp.arange(ROT // 2).astype(f32) / ROT)
    angles = jnp.arange(length, dtype=jnp.int32).astype(f32)[:, None] * frequency[None, :]
    spare = jnp.zeros((length, HEAD - ROT), f32)
    repeat = width // HEAD
    cos = jnp.tile(jnp.concatenate([jnp.cos(angles)] * 2 + [spare], axis=1), (1, repeat))
    sin = jnp.tile(jnp.concatenate([jnp.sin(angles)] * 2 + [spare], axis=1), (1, repeat))
    third = lambda which: pl.BlockSpec((length, width), lambda g: (0, which * groups + g))
    group = pl.BlockSpec((length, width), lambda g: (0, g))
    table = pl.BlockSpec((length, width), lambda g: (0, 0))
    out = jax.ShapeDtypeStruct((length, columns), bf16)
    if width < 128:
        parts = [hidden[:, k * columns : (k + 1) * columns] for k in range(3)]
        specs = [group] * 3
    else:
        parts = [hidden] * 3
        specs = [third(0), third(1), third(2)]
    pairs = length * length * columns // 2
    return pl.pallas_call(
        functools.partial(attention_kernel, length, width),
        grid=(groups,),
        in_specs=specs + [group, table, table],
        out_specs=[group] * 4,
        out_shape=[out] * 4,
        scratch_shapes=[
            pltpu.VMEM((length, width), bf16),
            pltpu.VMEM((length, width), bf16),
            pltpu.VMEM((length, width), bf16),
            pltpu.VMEM((width, length), bf16),
            pltpu.VMEM((width, length), bf16),
            pltpu.VMEM((length, width), f32),
            pltpu.VMEM((length, width), f32),
        ],
        compiler_params=pltpu.CompilerParams(vmem_limit_bytes=56 * 2**20),
        cost_estimate=pl.CostEstimate(
            flops=14 * pairs * 2, bytes_accessed=length * columns * 30, transcendentals=pairs // HEAD
        ),
        name="attention",
    )(*parts, grad_mix, cos, sin)


def shift_pairs(size, by):
    return [(k, (k + by) % size) for k in range(size)]


def flip_pairs(size, bit):
    return [(k, k ^ bit) for k in range(size)]


def gather_small(vector):
    held = vector[None]
    for axis in ("ctx", "dp"):
        size = lax.axis_size(axis)
        place = lax.axis_index(axis)
        bit = 1
        while bit < size:
            other = lax.ppermute(held, axis, flip_pairs(size, bit))
            upper = (place & bit) != 0
            held = jnp.where(
                upper, jnp.concatenate([other, held]), jnp.concatenate([held, other])
            )
            bit *= 2
    return held


def scatter_small(terms):
    held = terms
    for axis in ("dp", "ctx"):
        size = lax.axis_size(axis)
        place = lax.axis_index(axis)
        bit = size // 2
        while bit >= 1:
            half = held.shape[0] // 2
            low, high = held[:half], held[half:]
            upper = (place & bit) != 0
            other = lax.ppermute(jnp.where(upper, low, high), axis, flip_pairs(size, bit))
            held = jnp.where(upper, high, low) + other
            bit //= 2
    return held[0]


def put_rows(buffer, block, index, count):
    buffer = lax.dynamic_update_slice(buffer, block[:BLK], (index * BLK, 0))
    return lax.dynamic_update_slice(buffer, block[BLK:], ((2 * count - 1 - index) * BLK, 0))


def take_rows(array, index, count):
    former = lax.dynamic_slice_in_dim(array, index * BLK, BLK, 0)
    latter = lax.dynamic_slice_in_dim(array, (2 * count - 1 - index) * BLK, BLK, 0)
    return jnp.concatenate([former, latter], axis=0)


def gather_rows(block):
    count = lax.axis_size("ctx")
    place = lax.axis_index("ctx")
    far = count // 2
    total = jnp.zeros((count * 2 * BLK, block.shape[1]), block.dtype)
    held = block
    for step in range(far):
        if step:
            held = lax.ppermute(held, "ctx", shift_pairs(count, 2))
        owner = (place + count - 2 * step) % count
        other = lax.ppermute(held, "ctx", flip_pairs(count, 1))
        total = put_rows(total, held, owner, count)
        total = put_rows(total, other, owner ^ 1, count)
    return total


def scatter_rows(terms):
    count = lax.axis_size("ctx")
    place = lax.axis_index("ctx")
    far = count // 2
    total = None
    for step in [*range(1, far), 0]:
        owner = (place + 2 * step) % count
        other = lax.ppermute(
            take_rows(terms, owner ^ 1, count).astype(bf16), "ctx", flip_pairs(count, 1)
        )
        joint = take_rows(terms, owner, count) + other.astype(f32)
        if step:
            joint = lax.ppermute(joint.astype(bf16), "ctx", shift_pairs(count, 2 * step)).astype(f32)
        total = joint if total is None else total + joint
    return total


def column_pieces(index, count):
    own = D // count
    rows = (D + FF) // (4 * count)
    pieces = [(which * D + index * own, own) for which in range(3)]
    pieces.append((3 * D + index * (rows - own), rows - own))
    for part in range(1, 4):
        pieces.append((3 * D + part * rows * count - D + index * rows, rows))
    return pieces


def take_columns(array, index, count, pieces):
    parts = [
        lax.dynamic_slice_in_dim(array, start, width, 1)
        for start, width in column_pieces(index, count)[pieces]
    ]
    return jnp.concatenate(parts, axis=1)


def spread_columns(array, pieces):
    count = lax.axis_size("ctx")
    place = lax.axis_index("ctx")
    rows = array.shape[0]
    own = take_columns(array, place, count, pieces)
    total = jnp.zeros((count, rows, own.shape[1]), array.dtype)
    total = lax.dynamic_update_slice(total, own[None], (place, 0, 0))
    for step in range(1, count):
        sent = take_columns(array, (place + step) % count, count, pieces)
        got = lax.ppermute(sent, "ctx", shift_pairs(count, step))
        total = lax.dynamic_update_slice(total, got[None], ((place + count - step) % count, 0, 0))
    return total.reshape(count * rows, -1)


def collect_columns(output, array, pieces):
    count = lax.axis_size("ctx")
    place = lax.axis_index("ctx")
    rows = output.shape[0]

    def put(output, block, index):
        at = 0
        for start, width in column_pieces(index, count)[pieces]:
            output = lax.dynamic_update_slice(output, block[:, at : at + width], (0, start))
            at += width
        return output

    output = put(output, lax.dynamic_slice_in_dim(array, place * rows, rows, 0), place)
    for step in range(1, count):
        sent = lax.dynamic_slice_in_dim(array, ((place + step) % count) * rows, rows, 0)
        got = lax.ppermute(sent.astype(bf16), "ctx", shift_pairs(count, step))
        output = put(output, got.astype(f32), (place + count - step) % count)
    return output


def gather_dp(block):
    place = lax.axis_index("dp")
    rows = block.shape[0]
    total = jnp.zeros((4, *block.shape), block.dtype)
    across = lax.ppermute(block, "dp", flip_pairs(4, 2))
    total = lax.dynamic_update_slice(total, block[None], (place, 0, 0))
    total = lax.dynamic_update_slice(total, across[None], (place ^ 2, 0, 0))
    beside = lax.ppermute(block, "dp", flip_pairs(4, 1))
    total = lax.dynamic_update_slice(total, beside[None], (place ^ 1, 0, 0))
    beyond = lax.ppermute(across, "dp", flip_pairs(4, 1))
    total = lax.dynamic_update_slice(total, beyond[None], (place ^ 3, 0, 0))
    return total.reshape(4 * rows, -1)


def scatter_dp(terms):
    place = lax.axis_index("dp")
    rows = terms.shape[0] // 4
    part = lambda index: lax.dynamic_slice_in_dim(terms, index * rows, rows, 0)
    sent_far = part(place ^ 3).astype(bf16)
    got_far = lax.ppermute(sent_far, "dp", flip_pairs(4, 1))
    far = part(place ^ 2) + got_far.astype(f32)
    got_near = lax.ppermute(part(place ^ 1).astype(bf16), "dp", flip_pairs(4, 1))
    near = part(place) + got_near.astype(f32)
    got = lax.ppermute(far.astype(bf16), "dp", flip_pairs(4, 2))
    return near + got.astype(f32)


def unit_rounds(count):
    edges = []
    for m in range(5 * count):
        owner, slot = (m // 4, m % 4) if m < 4 * count else (m - 4 * count, 4)
        edges.append((m // 5, m % 5, owner, slot))
    rounds = []
    left = list(edges)
    for _ in range(5):
        by_source = [[e for e in left if e[0] == s] for s in range(count)]
        taken = {}

        def place_edge(source, seen):
            for edge in by_source[source]:
                if edge[2] in seen:
                    continue
                seen.add(edge[2])
                if edge[2] not in taken or place_edge(taken[edge[2]][0], seen):
                    taken[edge[2]] = edge
                    return True
            return False

        for source in range(count):
            assert place_edge(source, set())
        chosen = {edge[0]: edge for edge in taken.values()}
        rounds.append([chosen[s] for s in range(count)])
        for edge in taken.values():
            left.remove(edge)
    return rounds


def swap_units(block, back):
    count = lax.axis_size("ctx")
    place = lax.axis_index("ctx")
    first = lax.axis_index("dp") == 0
    rows = block.shape[0] // 5
    total = jnp.zeros_like(block)
    for chosen in unit_rounds(count):
        out_unit, in_unit, pairs = [0] * count, [0] * count, []
        for source, unit, owner, slot in chosen:
            if back:
                source, unit, owner, slot = owner, slot, source, unit
            pairs.append((source, owner))
            out_unit[source] = unit
            in_unit[owner] = slot
        sent = lax.dynamic_slice_in_dim(block, jnp.array(out_unit)[place] * rows, rows, 0)
        got = lax.ppermute(sent, ("dp", "ctx"), pairs)
        total = lax.dynamic_update_slice(total, got, (jnp.array(in_unit)[place] * rows, 0))
    return jnp.where(first, total, block)


def local(
    tokens, norm_gain, norm_shift, input_weight, input_bias, output_weight, output_bias, cotangent
):
    count = lax.axis_size("ctx")
    place = lax.axis_index("ctx")
    devices = 4 * count
    own = D // count
    qkv = slice(0, 3)
    mlp = slice(3, None)
    token_block = tokens.reshape(2 * BLK, D)
    grad_block = cotangent.reshape(2 * BLK, D)

    small = jnp.concatenate([norm_gain, norm_shift, input_bias, output_bias])
    params = gather_small(small).astype(f32)
    cuts = [norm_gain.shape[0], norm_shift.shape[0], input_bias.shape[0], output_bias.shape[0]]
    ends = [sum(cuts[: k + 1]) for k in range(4)]
    gain, shift, bias_in, bias_out = (
        params[:, end - cut : end].reshape(-1) for cut, end in zip(cuts, ends)
    )

    x = gather_rows(token_block).astype(f32)
    weight_mlp = gather_dp(spread_columns(input_weight, mlp))
    weight_qkv = gather_dp(spread_columns(input_weight, qkv))
    weight_out = gather_dp(swap_units(output_weight, False))
    grads = gather_rows(grad_block)

    middle = jnp.mean(x, axis=-1, keepdims=True)
    centred = x - middle
    spread = jnp.mean(centred * centred, axis=-1, keepdims=True)
    xhat = centred * lax.rsqrt(spread + epsilon)
    normed = (xhat * gain + shift).astype(bf16)

    bias_columns = take_columns(bias_in[None], place, count, slice(None))
    hidden_mlp = dot(normed, weight_mlp, ((1,), (0,))) + bias_columns[:, 3 * own :]
    hidden_qkv = dot(normed, weight_qkv, ((1,), (0,))) + bias_columns[:, : 3 * own]
    activated, gelu_back = jax.vjp(lambda v: jax.nn.gelu(v, approximate=True), hidden_mlp)

    grad_mix = dot(grads, weight_out[:own], ((1,), (1,))).astype(bf16)
    grad_mlp = dot(grads, weight_out[own:], ((1,), (1,)))
    (grad_up,) = gelu_back(grad_mlp)
    grad_up = grad_up.astype(bf16)

    attended, grad_q, grad_k, grad_v = attention(hidden_qkv, grad_mix)
    grad_qkv = jnp.concatenate([grad_q, grad_k, grad_v], axis=1)
    branch = jnp.concatenate([attended, activated.astype(bf16)], axis=1)

    partial_out = dot(branch, weight_out, ((1,), (0,)))
    block_out = (
        (token_block.astype(f32) + scatter_rows(partial_out) + bias_out)
        .astype(bf16)
        .reshape(tokens.shape)
    )

    weight_out_term = dot(branch, grads, ((0,), (0,)))
    weightout_grad = swap_units(scatter_dp(weight_out_term).astype(bf16), True).astype(f32)

    weight_mlp_term = dot(normed, grad_up, ((0,), (0,)))
    weight_qkv_term = dot(normed, grad_qkv, ((0,), (0,)))
    weightin_grad = jnp.zeros(input_weight.shape, f32)
    weightin_grad = collect_columns(weightin_grad, scatter_dp(weight_mlp_term), mlp)
    weightin_grad = collect_columns(weightin_grad, scatter_dp(weight_qkv_term), qkv)

    grad_normed = dot(grad_qkv, weight_qkv, ((1,), (1,))) + dot(grad_up, weight_mlp, ((1,), (1,)))
    gain_term = jnp.sum(grad_normed * xhat, axis=0)
    shift_term = jnp.sum(grad_normed, axis=0)
    bias_in_term = jnp.concatenate(
        [jnp.sum(grad_qkv.astype(f32), axis=0), jnp.sum(grad_up.astype(f32), axis=0)]
    )
    bias_in_all = jnp.zeros((3 * D + FF,), f32)
    at = 0
    for start, width in column_pieces(place, count):
        bias_in_all = lax.dynamic_update_slice(bias_in_all, bias_in_term[at : at + width], (start,))
        at += width
    bias_out_term = jnp.sum(grad_block.astype(f32), axis=0)
    small_terms = jnp.concatenate(
        [
            gain_term.reshape(devices, -1),
            shift_term.reshape(devices, -1),
            bias_in_all.reshape(devices, -1),
            bias_out_term.reshape(devices, -1),
        ],
        axis=1,
    )
    small_grads = scatter_small(small_terms)
    gain_grad, shift_grad, biasin_grad, biasout_grad = (
        small_grads[end - cut : end] for cut, end in zip(cuts, ends)
    )

    own_normed = scatter_rows(grad_normed)
    own_x = token_block.astype(f32)
    own_centred = own_x - jnp.mean(own_x, axis=-1, keepdims=True)
    own_scale = lax.rsqrt(jnp.mean(own_centred * own_centred, axis=-1, keepdims=True) + epsilon)
    own_hat = own_centred * own_scale
    g = own_normed * gain
    tokens_grad = grad_block.astype(f32) + own_scale * (
        g
        - jnp.mean(g, axis=-1, keepdims=True)
        - own_hat * jnp.mean(g * own_hat, axis=-1, keepdims=True)
    )
    return (
        block_out,
        tokens_grad.reshape(tokens.shape),
        gain_grad,
        shift_grad,
        weightin_grad,
        biasin_grad,
        weightout_grad,
        biasout_grad,
    )


def solution(mesh):
    placed = (
        P("dp", None, "ctx", None, None),
        P(("dp", "ctx")),
        P(("dp", "ctx")),
        P(("dp", "ctx"), None),
        P(("dp", "ctx")),
        P(("dp", "ctx"), None),
        P(("dp", "ctx")),
        P("dp", None, "ctx", None, None),
    )
    return jax.shard_map(
        local,
        mesh=mesh,
        in_specs=placed,
        out_specs=(
            P("dp", None, "ctx", None, None),
            P("dp", None, "ctx", None, None),
            P(("dp", "ctx")),
            P(("dp", "ctx")),
            P(("dp", "ctx"), None),
            P(("dp", "ctx")),
            P(("dp", "ctx"), None),
            P(("dp", "ctx")),
        ),
        check_vma=False,
    )
```

time: 5620 us -> 702 us (0.12)
  the two profiles are of different devices: /device:TPU:0 before, /device:TPU:24 now
where the time goes in v1:
time: 702 us; the launch traced here: 691 us
  waiting for transfers between devices  224 us (32%)
  local copies, waits for them, and re-layouts  170 us (24%)
  starting transfers between devices  145 us (21%)
  matrix products  68.6 us (10%)
  other arithmetic  56 us (8%)
  Pallas kernels  17.1 us (2%)
  between operations  9.36 us (1%)
    dynamic_update_slice x56, local copies, waits for them, and re-layouts, put(): lax.dynamic_update_slice(output, block[:, at:at + width], (0, start))  70.6 us
    dot_general x10, matrix products, dot(): return lax.dot_general(a, b, (dims, ((), ())), preferred_element_type=f32)  68.6 us
    ppermute x8, waiting for transfers between devices, gather_rows(): other = lax.ppermute(held, 'ctx', flip_pairs(count, 1))  55.5 us
    ppermute x6, waiting for transfers between devices, scatter_rows(): lax.ppermute(joint.astype(bf16), 'ctx', shift_pairs(count, 2 * step))  38.6 us
    ppermute x14, waiting for transfers between devices, spread_columns(): got = lax.ppermute(sent, 'ctx', shift_pairs(count, step))  34.9 us
    ppermute x14, starting transfers between devices, collect_columns(): got = lax.ppermute(sent.astype(bf16), 'ctx', shift_pairs(count, step))  32.5 us
    ppermute x10, starting transfers between devices, swap_units(): got = lax.ppermute(sent, ('dp', 'ctx'), pairs)  29.4 us
    ppermute x6, waiting for transfers between devices, gather_rows(): held = lax.ppermute(held, 'ctx', shift_pairs(count, 2))  26.6 us
  transfers between devices with their start and end apart: 94, of which 38 were waited for; matrix products, arithmetic and copies ran while one was open for 32% of the time, Pallas kernels for 0%

profile of v1, /device:TPU:24, one launch (start us, length us, event | category | flops | bytes accessed | tf_op | source)
XLA Modules:
  0.0 690.6 jit_solution(2886324434602880706)
XLA Ops:
  160.7 6.5 collective-permute-done.33
  183.6 12.1 %collective-permute-done.2 = bf16[128,2048]{1,0:T(8,128)(2,1)S(1)} collective-permute-done((bf16[128,2048]{1,0:T(8,128)(2,1)}, bf16[128,2048]{1,0:T(8,128)(2,1)S(1)}, u32[]{:S(2)}, u32[]{:S(2)}) %collective-permute-start.2) | collective-permute-done | bytes 524320 | tf_op jit(solution)/shard_map/ppermute | solution.py:216
  197.1 8.9 %collective-permute-done.24 = bf16[128,2048]{1,0:T(8,128)(2,1)S(1)} collective-permute-done((bf16[128,2048]{1,0:T(8,128)(2,1)S(1)}, bf16[128,2048]{1,0:T(8,128)(2,1)S(1)}, u32[]{:S(2)}, u32[]{:S(2)}) %collective-permute-start.24) | collective-permute-done | bytes 524320 | tf_op jit(solution)/shard_map/ppermute | solution.py:216
  207.4 10.9 %collective-permute-done.3 = bf16[128,2048]{1,0:T(8,128)(2,1)S(1)} collective-permute-done((bf16[128,2048]{1,0:T(8,128)(2,1)}, bf16[128,2048]{1,0:T(8,128)(2,1)S(1)}, u32[]{:S(2)}, u32[]{:S(2)}) %collective-permute-start.3) | collective-permute-done | bytes 524320 | tf_op jit(solution)/shard_map/ppermute | solution.py:214
  219.7 7.8 %collective-permute-done.25 = bf16[128,2048]{1,0:T(8,128)(2,1)S(1)} collective-permute-done((bf16[128,2048]{1,0:T(8,128)(2,1)S(1)}, bf16[128,2048]{1,0:T(8,128)(2,1)S(1)}, u32[]{:S(2)}, u32[]{:S(2)}) %collective-permute-start.25) | collective-permute-done | bytes 524320 | tf_op jit(solution)/shard_map/ppermute | solution.py:214
  231.4 11.8 %collective-permute-done.4 = bf16[128,2048]{1,0:T(8,128)(2,1)S(1)} collective-permute-done((bf16[128,2048]{1,0:T(8,128)(2,1)S(1)}, bf16[128,2048]{1,0:T(8,128)(2,1)S(1)}, u32[]{:S(2)}, u32[]{:S(2)}) %collective-permute-start.4) | collective-permute-done | bytes 524320 | tf_op jit(solution)/shard_map/ppermute | solution.py:216
  244.9 11.8 %collective-permute-done.26 = bf16[128,2048]{1,0:T(8,128)(2,1)S(1)} collective-permute-done((bf16[128,2048]{1,0:T(8,128)(2,1)S(1)}, bf16[128,2048]{1,0:T(8,128)(2,1)S(1)}, u32[]{:S(2)}, u32[]{:S(2)}) %collective-permute-start.26) | collective-permute-done | bytes 524320 | tf_op jit(solution)/shard_map/ppermute | solution.py:216
  261.5 7.9 %collective-permute-done.27 = bf16[128,2048]{1,0:T(8,128)(2,1)S(1)} collective-permute-done((bf16[128,2048]{1,0:T(8,128)(2,1)S(1)}, bf16[128,2048]{1,0:T(8,128)(2,1)S(1)}, u32[]{:S(2)}, u32[]{:S(2)}) %collective-permute-start.27) | collective-permute-done | bytes 524320 | tf_op jit(solution)/shard_map/ppermute | solution.py:214
  273.4 10.9 %collective-permute-done.6 = bf16[128,2048]{1,0:T(8,128)(2,1)S(1)} collective-permute-done((bf16[128,2048]{1,0:T(8,128)(2,1)S(1)}, bf16[128,2048]{1,0:T(8,128)(2,1)S(1)}, u32[]{:S(2)}, u32[]{:S(2)}) %collective-permute-start.6) | collective-permute-done | bytes 524320 | tf_op jit(solution)/shard_map/ppermute | solution.py:216
  302.6 6.6 multiply_convert_fusion
  313.7 9.7 %convert_reduce_fusion.1 = (f32[1024]{0:T(1024)S(1)}, bf16[1024,1024]{1,0:T(8,128)(2,1)S(1)}) fusion(f32[1024,1024]{1,0:T(8,128)S(1)} %get-tuple-element.200, f32[1024]{0:T(1024)S(1)} %bitcast.143, bf16[1024,2048]{1,0:T(8,128)(2,1)} %slice_dynamic-update-slice_fusion, bf16[1280,2048]{1,0:T(8,128)(2,1)S(1)} %bitcast.126), kind=kOutput, calls=%fused_computation.21 | convolution fusion | flops 4319083520 | bytes 14688256 | tf_op jit(solution)/shard_map/dot_general | solution.py:27
  323.4 6.8 fusion.59
  330.1 6.8 fusion.60
  336.9 17.1 %attention.1 = (bf16[1024,256]{1,0:T(8,128)(2,1)}, bf16[1024,256]{1,0:T(8,128)(2,1)}, bf16[1024,256]{1,0:T(8,128)(2,1)}, bf16[1024,256]{1,0:T(8,128)(2,1)}) custom-call(f32[1024,768]{1,0:T(8,128)} %convolution_add_fusion.1.hq.hk.hv, f32[1024,768]{1,0:T(8,128)} %convolution_add_fusion.1.hq.hk.hv, f32[1024,768]{1,0:T(8,128)} %convolution_add_fusion.1.hq.hk.hv, ...), custom_call_target="tpu_custom_call" | custom-call | flops 3758096384 | bytes 7864320 | tf_op jit(solution)/shard_map/attention/pallas_call | solution.py:132
  369.1 10.6 %fusion.19 = f32[1280,2048]{1,0:T(8,128)} fusion(bf16[1024,2048]{1,0:T(8,128)(2,1)} %slice_dynamic-update-slice_fusion, bf16[1024,1024]{1,0:T(8,128)(2,1)S(1)} %copy-done.53, bf16[1024,256]{1,0:T(8,128)(2,1)S(1)} %copy-done.54), kind=kOutput, calls=%fused_computation.35 | convolution fusion | flops 5373952000 | bytes 17301504 | tf_op jit(solution)/shard_map/dot_general | solution.py:27
  379.7 7.5 %fusion.6 = (f32[2048]{0:T(1024)S(1)}, f32[2048]{0:T(1024)S(1)}, f32[1024,2048]{1,0:T(8,128)S(1)}) fusion(bf16[1024,2048]{1,0:T(8,128)(2,1)} %slice_dynamic-update-slice_fusion.14, f32[1024]{0:T(1024)S(1)} %add_rsqrt_fusion, f32[1024]{0:T(1024)S(1)} %broadcast_multiply_fusion, f32[1024,2048]{1,0:T(8,128)} %fusion.59, bf16[1024,768]{1,0:T(8,128)(2,1)} %copy-done.8, ...), kind=kOutput, calls=%fused_computation.8 | convolution fusion | flops 3235901440 | bytes 25714688 | tf_op jit(solution)/shard_map/dot_general | solution.py:27
  425.2 14.0 %collective-permute-done.65 = f32[1,640]{1,0:T(1,128)S(1)} collective-permute-done((f32[1,640]{1,0:T(1,128)S(1)}, f32[1,640]{1,0:T(1,128)S(1)}, u32[]{:S(2)}, u32[]{:S(2)}) %collective-permute-start.65) | collective-permute-done | bytes 2592 | tf_op jit(solution)/shard_map/ppermute | solution.py:189
  446.7 7.5 %collective-permute-done.51 = bf16[128,2048]{1,0:T(8,128)(2,1)S(1)} collective-permute-done((bf16[128,2048]{1,0:T(8,128)(2,1)S(1)}, bf16[128,2048]{1,0:T(8,128)(2,1)S(1)}, u32[]{:S(2)}, u32[]{:S(2)}) %collective-permute-start.51) | collective-permute-done | bytes 524320 | tf_op jit(solution)/shard_map/ppermute | solution.py:229
  455.6 7.6 %collective-permute-done.49 = bf16[128,2048]{1,0:T(8,128)(2,1)S(1)} collective-permute-done((bf16[128,2048]{1,0:T(8,128)(2,1)S(1)}, bf16[128,2048]{1,0:T(8,128)(2,1)S(1)}, u32[]{:S(2)}, u32[]{:S(2)}) %collective-permute-start.49) | collective-permute-done | bytes 524320 | tf_op jit(solution)/shard_map/ppermute | solution.py:229
  475.5 10.6 %collective-permute-done.57 = bf16[128,2048]{1,0:T(8,128)(2,1)S(1)} collective-permute-done((bf16[128,2048]{1,0:T(8,128)(2,1)S(1)}, bf16[128,2048]{1,0:T(8,128)(2,1)S(1)}, u32[]{:S(2)}, u32[]{:S(2)}) %collective-permute-start.57) | collective-permute-done | bytes 524320 | tf_op jit(solution)/shard_map/ppermute | solution.py:234
  488.6 10.6 %collective-permute-start.52 = (bf16[128,2048]{1,0:T(8,128)(2,1)S(1)}, bf16[128,2048]{1,0:T(8,128)(2,1)S(1)}, u32[]{:S(2)}, u32[]{:S(2)}) collective-permute-start(bf16[128,2048]{1,0:T(8,128)(2,1)S(1)} %fusion.35), channel_id=1, source_target_pairs={{0,6},{1,7},{2,0},{3,1},{4,2},{5,3},{6,4},{7,5},{8,14},{9,15},{10,... | collective-permute-start | bytes 1572872 | tf_op jit(solution)/shard_map/ppermute | solution.py:234
  511.9 21.8 %collective-permute-done.50 = bf16[128,2048]{1,0:T(8,128)(2,1)S(1)} collective-permute-done((bf16[128,2048]{1,0:T(8,128)(2,1)S(1)}, bf16[128,2048]{1,0:T(8,128)(2,1)S(1)}, u32[]{:S(2)}, u32[]{:S(2)}) %collective-permute-start.50) | collective-permute-done | bytes 524320 | tf_op jit(solution)/shard_map/ppermute | solution.py:234
  540.2 14.3 %collective-permute-start.80 = (bf16[64,768]{1,0:T(8,128)(2,1)S(1)}, bf16[64,768]{1,0:T(8,128)(2,1)S(1)}, u32[]{:S(2)}, u32[]{:S(2)}) collective-permute-start(bf16[64,768]{1,0:T(8,128)(2,1)S(1)} %get-tuple-element.148), channel_id=1, source_target_pairs={{0,2},{1,3},{2,4},{3,5},{4,6},{5,7},{6,0},{7,1},{8,10},{9,11},{10,... | collective-permute-start | bytes 294920 | tf_op jit(solution)/shard_map/ppermute | solution.py:286
  561.9 7.6 %collective-permute-done.81 = bf16[64,768]{1,0:T(8,128)(2,1)S(1)} collective-permute-done((bf16[64,768]{1,0:T(8,128)(2,1)S(1)}, bf16[64,768]{1,0:T(8,128)(2,1)S(1)}, u32[]{:S(2)}, u32[]{:S(2)}) %collective-permute-start.81) | collective-permute-done | bytes 98336 | tf_op jit(solution)/shard_map/ppermute | solution.py:286
  (587 shorter events, 433.6 us)
Async XLA Ops:
  0.7 167.8 %collective-permute-start = (bf16[128,2048]{1,0:T(8,128)(2,1)}, bf16[128,2048]{1,0:T(8,128)(2,1)}, u32[]{:S(2)}, u32[]{:S(2)}) collective-permute-start(bf16[128,2048]{1,0:T(8,128)(2,1)} %bitcast.123), channel_id=1, source_target_pairs={{0,1},{1,0},{2,3},{3,2},{4,5},{5,4},{6,7},{7,6},{8,9},{9,8},{10,11... | collective-permute-start | bytes 1572872 | tf_op jit(solution)/shard_map/ppermute | solution.py:216
  2.3 173.1 %collective-permute-start.1 = (bf16[128,2048]{1,0:T(8,128)(2,1)}, bf16[128,2048]{1,0:T(8,128)(2,1)}, u32[]{:S(2)}, u32[]{:S(2)}) collective-permute-start(bf16[128,2048]{1,0:T(8,128)(2,1)} %bitcast.124), channel_id=1, source_target_pairs={{0,2},{1,3},{2,4},{3,5},{4,6},{5,7},{6,0},{7,1},{8,10},{9,11},{10,... | collective-permute-start | bytes 1572872 | tf_op jit(solution)/shard_map/ppermute | solution.py:214
  3.9 43.8 %collective-permute-start.7 = (bf16[1,640]{1,0:T(2,128)(2,1)}, bf16[1,640]{1,0:T(2,128)(2,1)}, u32[]{:S(2)}, u32[]{:S(2)}) collective-permute-start(bf16[1,640]{1,0:T(2,128)(2,1)} %broadcast_in_dim.113), channel_id=1, source_target_pairs={{0,1},{1,0},{2,3},{3,2},{4,5},{5,4},{6,7},{7,6},{8,9},{9,8},{10,11... | collective-permute-start | bytes 3848 | tf_op jit(solution)/shard_map/ppermute | solution.py:170
  10.0 114.0 %collective-permute-start.37 = (bf16[64,1024]{1,0:T(8,128)(2,1)}, bf16[64,1024]{1,0:T(8,128)(2,1)}, u32[]{:S(2)}, u32[]{:S(2)}) collective-permute-start(bf16[64,1024]{1,0:T(8,128)(2,1)} %pad_maximum_fusion.11), channel_id=1, source_target_pairs={{0,1},{1,2},{2,3},{3,4},{4,5},{5,6},{6,7},{7,0},{8,9},{9,10},{10,1... | collective-permute-start | bytes 393224 | tf_op jit(solution)/shard_map/ppermute | solution.py:266
  12.5 116.1 %collective-permute-start.38 = (bf16[64,1024]{1,0:T(8,128)(2,1)}, bf16[64,1024]{1,0:T(8,128)(2,1)}, u32[]{:S(2)}, u32[]{:S(2)}) collective-permute-start(bf16[64,1024]{1,0:T(8,128)(2,1)} %pad_maximum_fusion.12), channel_id=1, source_target_pairs={{0,2},{1,3},{2,4},{3,5},{4,6},{5,7},{6,0},{7,1},{8,10},{9,11},{10,... | collective-permute-start | bytes 393224 | tf_op jit(solution)/shard_map/ppermute | solution.py:266
  136.3 35.6 %collective-permute-start.22 = (bf16[128,2048]{1,0:T(8,128)(2,1)S(1)}, bf16[128,2048]{1,0:T(8,128)(2,1)S(1)}, u32[]{:S(2)}, u32[]{:S(2)}) collective-permute-start(bf16[128,2048]{1,0:T(8,128)(2,1)S(1)} %bitcast.128), channel_id=1, source_target_pairs={{0,1},{1,0},{2,3},{3,2},{4,5},{5,4},{6,7},{7,6},{8,9},{9,8},{10,11... | collective-permute-start | bytes 1572872 | tf_op jit(solution)/shard_map/ppermute | solution.py:216
  171.9 57.0 %collective-permute-start.44 = (bf16[512,1024]{1,0:T(8,128)(2,1)}, bf16[512,1024]{1,0:T(8,128)(2,1)S(1)}, u32[]{:S(2)}, u32[]{:S(2)}) collective-permute-start(bf16[512,1024]{1,0:T(8,128)(2,1)} %bitcast.46), channel_id=1, source_target_pairs={{0,16},{8,24},{16,0},{24,8},{1,17},{9,25},{17,1},{25,9},{2,18},{10... | collective-permute-start | bytes 3145736 | tf_op jit(solution)/shard_map/ppermute | solution.py:295
  175.4 53.9 %collective-permute-start.45 = (bf16[512,1024]{1,0:T(8,128)(2,1)}, bf16[512,1024]{1,0:T(8,128)(2,1)S(1)}, u32[]{:S(2)}, u32[]{:S(2)}) collective-permute-start(bf16[512,1024]{1,0:T(8,128)(2,1)} %bitcast.46), channel_id=1, source_target_pairs={{0,8},{8,0},{16,24},{24,16},{1,9},{9,1},{17,25},{25,17},{2,10},{10... | collective-permute-start | bytes 3145736 | tf_op jit(solution)/shard_map/ppermute | solution.py:298
  178.9 92.3 %collective-permute-start.34 = (bf16[320,2048]{1,0:T(8,128)(2,1)S(1)}, bf16[320,2048]{1,0:T(8,128)(2,1)S(1)}, u32[]{:S(2)}, u32[]{:S(2)}) collective-permute-start(bf16[320,2048]{1,0:T(8,128)(2,1)S(1)} %get-tuple-element.38), channel_id=1, source_target_pairs={{0,16},{8,24},{16,0},{24,8},{1,17},{9,25},{17,1},{25,9},{2,18},{10... | collective-permute-start | bytes 3932168 | tf_op jit(solution)/shard_map/ppermute | solution.py:295
  183.4 89.7 %collective-permute-start.35 = (bf16[320,2048]{1,0:T(8,128)(2,1)S(1)}, bf16[320,2048]{1,0:T(8,128)(2,1)S(1)}, u32[]{:S(2)}, u32[]{:S(2)}) collective-permute-start(bf16[320,2048]{1,0:T(8,128)(2,1)S(1)} %get-tuple-element.38), channel_id=1, source_target_pairs={{0,8},{8,0},{16,24},{24,16},{1,9},{9,1},{17,25},{25,17},{2,10},{10... | collective-permute-start | bytes 3932168 | tf_op jit(solution)/shard_map/ppermute | solution.py:298
  227.4 45.9 %collective-permute-start.21 = (bf16[512,768]{1,0:T(8,128)(2,1)S(1)}, bf16[512,768]{1,0:T(8,128)(2,1)S(1)}, u32[]{:S(2)}, u32[]{:S(2)}) collective-permute-start(bf16[512,768]{1,0:T(8,128)(2,1)S(1)} %collective-permute-done.19), channel_id=1, source_target_pairs={{0,8},{8,0},{16,24},{24,16},{1,9},{9,1},{17,25},{25,17},{2,10},{10... | collective-permute-start | bytes 2359304 | tf_op jit(solution)/shard_map/ppermute | solution.py:300
  260.0 42.4 %collective-permute-start.46 = (bf16[512,1024]{1,0:T(8,128)(2,1)S(1)}, bf16[512,1024]{1,0:T(8,128)(2,1)S(1)}, u32[]{:S(2)}, u32[]{:S(2)}) collective-permute-start(bf16[512,1024]{1,0:T(8,128)(2,1)S(1)} %collective-permute-done.44), channel_id=1, source_target_pairs={{0,8},{8,0},{16,24},{24,16},{1,9},{9,1},{17,25},{25,17},{2,10},{10... | collective-permute-start | bytes 3145736 | tf_op jit(solution)/shard_map/ppermute | solution.py:300
  273.1 36.1 %collective-permute-start.36 = (bf16[320,2048]{1,0:T(8,128)(2,1)S(1)}, bf16[320,2048]{1,0:T(8,128)(2,1)S(1)}, u32[]{:S(2)}, u32[]{:S(2)}) collective-permute-start(bf16[320,2048]{1,0:T(8,128)(2,1)S(1)} %collective-permute-done.34), channel_id=1, source_target_pairs={{0,8},{8,0},{16,24},{24,16},{1,9},{9,1},{17,25},{25,17},{2,10},{10... | collective-permute-start | bytes 3932168 | tf_op jit(solution)/shard_map/ppermute | solution.py:300
  393.3 73.9 %collective-permute-start.60 = (bf16[128,2048]{1,0:T(8,128)(2,1)}, bf16[128,2048]{1,0:T(8,128)(2,1)}, u32[]{:S(2)}, u32[]{:S(2)}) collective-permute-start(bf16[128,2048]{1,0:T(8,128)(2,1)} %pad_maximum_fusion.10), channel_id=1, source_target_pairs={{0,1},{1,0},{2,3},{3,2},{4,5},{5,4},{6,7},{7,6},{8,9},{9,8},{10,11... | collective-permute-start | bytes 1572872 | tf_op jit(solution)/shard_map/ppermute | solution.py:229
  394.5 46.4 %collective-permute-start.58 = (bf16[128,2048]{1,0:T(8,128)(2,1)}, bf16[128,2048]{1,0:T(8,128)(2,1)}, u32[]{:S(2)}, u32[]{:S(2)}) collective-permute-start(bf16[128,2048]{1,0:T(8,128)(2,1)} %pad_maximum_fusion.9), channel_id=1, source_target_pairs={{0,1},{1,0},{2,3},{3,2},{4,5},{5,4},{6,7},{7,6},{8,9},{9,8},{10,11... | collective-permute-start | bytes 1572872 | tf_op jit(solution)/shard_map/ppermute | solution.py:229
  397.0 46.7 %collective-permute-start.56 = (bf16[128,2048]{1,0:T(8,128)(2,1)}, bf16[128,2048]{1,0:T(8,128)(2,1)}, u32[]{:S(2)}, u32[]{:S(2)}) collective-permute-start(bf16[128,2048]{1,0:T(8,128)(2,1)} %pad_maximum_fusion.8), channel_id=1, source_target_pairs={{0,1},{1,0},{2,3},{3,2},{4,5},{5,4},{6,7},{7,6},{8,9},{9,8},{10,11... | collective-permute-start | bytes 1572872 | tf_op jit(solution)/shard_map/ppermute | solution.py:229
  398.3 47.1 %collective-permute-start.54 = (bf16[128,2048]{1,0:T(8,128)(2,1)}, bf16[128,2048]{1,0:T(8,128)(2,1)}, u32[]{:S(2)}, u32[]{:S(2)}) collective-permute-start(bf16[128,2048]{1,0:T(8,128)(2,1)} %pad_maximum_fusion.7), channel_id=1, source_target_pairs={{0,1},{1,0},{2,3},{3,2},{4,5},{5,4},{6,7},{7,6},{8,9},{9,8},{10,11... | collective-permute-start | bytes 1572872 | tf_op jit(solution)/shard_map/ppermute | solution.py:229
  486.2 68.3 %collective-permute-start.87 = (bf16[320,2048]{1,0:T(8,128)(2,1)S(1)}, bf16[320,2048]{1,0:T(8,128)(2,1)S(1)}, u32[]{:S(2)}, u32[]{:S(2)}) collective-permute-start(bf16[320,2048]{1,0:T(8,128)(2,1)S(1)} %get-tuple-element.40), channel_id=1, source_target_pairs={{0,8},{8,0},{16,24},{24,16},{1,9},{9,1},{17,25},{25,17},{2,10},{10... | collective-permute-start | bytes 3932168 | tf_op jit(solution)/shard_map/ppermute | solution.py:310
  499.6 40.6 %collective-permute-start.48 = (bf16[128,2048]{1,0:T(8,128)(2,1)S(1)}, bf16[128,2048]{1,0:T(8,128)(2,1)S(1)}, u32[]{:S(2)}, u32[]{:S(2)}) collective-permute-start(bf16[128,2048]{1,0:T(8,128)(2,1)S(1)} %fusion.33), channel_id=1, source_target_pairs={{0,2},{1,3},{2,4},{3,5},{4,6},{5,7},{6,0},{7,1},{8,10},{9,11},{10,... | collective-permute-start | bytes 1572872 | tf_op jit(solution)/shard_map/ppermute | solution.py:234
  503.6 53.3 %collective-permute-start.79 = (bf16[64,768]{1,0:T(8,128)(2,1)S(1)}, bf16[64,768]{1,0:T(8,128)(2,1)S(1)}, u32[]{:S(2)}, u32[]{:S(2)}) collective-permute-start(bf16[64,768]{1,0:T(8,128)(2,1)S(1)} %get-tuple-element.149), channel_id=1, source_target_pairs={{0,1},{1,2},{2,3},{3,4},{4,5},{5,6},{6,7},{7,0},{8,9},{9,10},{10,1... | collective-permute-start | bytes 294920 | tf_op jit(solution)/shard_map/ppermute | solution.py:286
  511.9 64.8 %collective-permute-start.66 = (bf16[512,1024]{1,0:T(8,128)(2,1)S(1)}, bf16[512,1024]{1,0:T(8,128)(2,1)S(1)}, u32[]{:S(2)}, u32[]{:S(2)}) collective-permute-start(bf16[512,1024]{1,0:T(8,128)(2,1)S(1)} %get-tuple-element.41), channel_id=1, source_target_pairs={{0,8},{8,0},{16,24},{24,16},{1,9},{9,1},{17,25},{25,17},{2,10},{10... | collective-permute-start | bytes 3145736 | tf_op jit(solution)/shard_map/ppermute | solution.py:312
  533.7 43.0 %collective-permute-start.68 = (bf16[512,1024]{1,0:T(8,128)(2,1)S(1)}, bf16[512,1024]{1,0:T(8,128)(2,1)S(1)}, u32[]{:S(2)}, u32[]{:S(2)}) collective-permute-start(bf16[512,1024]{1,0:T(8,128)(2,1)S(1)} %add_convert_fusion.2), channel_id=1, source_target_pairs={{0,16},{8,24},{16,0},{24,8},{1,17},{9,25},{17,1},{25,9},{2,18},{10... | collective-permute-start | bytes 3145736 | tf_op jit(solution)/shard_map/ppermute | solution.py:314
  574.8 87.4 %collective-permute-start.86 = (bf16[320,2048]{1,0:T(8,128)(2,1)}, bf16[320,2048]{1,0:T(8,128)(2,1)}, u32[]{:S(2)}, u32[]{:S(2)}) collective-permute-start(bf16[320,2048]{1,0:T(8,128)(2,1)} %get-tuple-element.39), channel_id=1, source_target_pairs={{0,8},{8,0},{16,24},{24,16},{1,9},{9,1},{17,25},{25,17},{2,10},{10... | collective-permute-start | bytes 3932168 | tf_op jit(solution)/shard_map/ppermute | solution.py:312
  576.6 85.6 %collective-permute-start.88 = (bf16[320,2048]{1,0:T(8,128)(2,1)}, bf16[320,2048]{1,0:T(8,128)(2,1)}, u32[]{:S(2)}, u32[]{:S(2)}) collective-permute-start(bf16[320,2048]{1,0:T(8,128)(2,1)} %add_convert_fusion.1), channel_id=1, source_target_pairs={{0,16},{8,24},{16,0},{24,8},{1,17},{9,25},{17,1},{25,9},{2,18},{10... | collective-permute-start | bytes 3932168 | tf_op jit(solution)/shard_map/ppermute | solution.py:314
  (129 other events, 2267.1 us)
